TPU v7x, 128 devices: a whole 4x4x4 slice. The times are simulated.
128 devices in a mesh: year: 8 (over x, core), date: 8 (over z_hi, y), pix: 2 (over z_lo).
Axes of the slice: x: 4, y: 4, z: 4 (z_hi: 2, z_lo: 2; z = z_hi * 2 + z_lo), core: 2. Of those that a mesh axis runs over, the one named last changes fastest.
Arguments:
- predicted_anomaly: bfloat16 [16, 8, 4, 83, 16384], P('year', 'date', None, None, 'pix'), may hold values from -6 to 6
- measured_anomaly: bfloat16 [16, 8, 4, 83, 16384], P('year', 'date', None, None, 'pix'), may hold values from -6 to 6
- filled_calendar: int32 [8], P('date'), may hold values from 1 to 4, 20 in all
Outputs:
- mean_error_field: float32 [8, 83, 2, 8192], P('date', None, 'pix', 'year')
- acc_map: float32 [83, 2, 8192], P(None, 'pix', ('year', 'date'))
- rmse_map: float32 [83, 2, 8192], P(None, 'pix', ('year', 'date'))
- scores: float32 [2, 83], replicated
Inputs may be any that keep to these rules, and one draw needn't show every extreme that they name: `filled_calendar`: counts sum to 20, and some window uses all 4 slots.
All inputs are finite; a program needn't handle non-finite values. No bound on the sum of `filled_calendar` on one device may be relied on, other than what follows from the above.
Results may differ from a plain program's by a relative error of at most 0.0003.
Values sent between devices are 32-bit elements; how exact they have to be, the bound alone decides.
A program may use at most 128 MiB of HBM per device.

v0:
```python
import functools
import math

import jax
import jax.numpy as jnp
from jax import lax
from jax.sharding import Mesh
from jax.sharding import PartitionSpec as P

YEAR = ("year_0", "year_1")
DATE = ("date_0", "date_1")
YEAR_DATE_PIX = ("year_0", "year_1", "date_0", "date_1", "pix")
YEAR_DATE = ("year_0", "year_1", "date_0", "date_1")


def copy_for_each(x, axis):
    copies = jnp.broadcast_to(x, (lax.axis_size(axis), *x.shape))
    return lax.all_to_all(copies, axis, split_axis=0, concat_axis=0, tiled=True)


def over_copies(x, axis):
    return copy_for_each(x, axis).sum(axis=0)


def one_axis_at_a_time(x, axes):
    return functools.reduce(lax.psum, axes, x)


def body(predicted_anomaly, measured_anomaly, filled_calendar):
    predicted_portion = predicted_anomaly[:, 0]
    o_local = measured_anomaly[:, 0]
    hindcast_portion, calendar_limit, variable_group, grid_points = predicted_portion.shape
    count = filled_calendar[0]
    n_year = lax.axis_size(YEAR)
    n_date = lax.axis_size(DATE)
    valid = (jnp.arange(calendar_limit, dtype=jnp.int32) < count).astype(jnp.float32)
    denom = hindcast_portion * n_year * count.astype(jnp.float32)
    weighting = valid[None, :, None, None]
    predicted_broad = predicted_portion.astype(jnp.float32)
    owide = o_local.astype(jnp.float32)
    fmask = weighting * predicted_broad
    omask = weighting * owide
    raw = jnp.stack(
        [
            jnp.sum(fmask, axis=(0, 1)),
            jnp.sum(omask, axis=(0, 1)),
            jnp.sum(fmask * predicted_broad, axis=(0, 1)),
            jnp.sum(fmask * owide, axis=(0, 1)),
            jnp.sum(omask * owide, axis=(0, 1)),
        ]
    )
    gathered_raw = lax.psum_scatter(raw, YEAR, scatter_dimension=2, tiled=True)
    sum_f = gathered_raw[0]
    sum_o = gathered_raw[1]
    sum_ff = gathered_raw[2]
    sum_fo = gathered_raw[3]
    sum_oo = gathered_raw[4]
    bias_share = (sum_f - sum_o) / denom
    shifted = bias_share * bias_share * denom
    mom_fo = sum_fo - bias_share * sum_o
    mom_ff = sum_ff - 2.0 * bias_share * sum_f + shifted
    mom_ee = sum_ff - 2.0 * sum_fo + sum_oo - 2.0 * bias_share * (sum_f - sum_o) + shifted
    stacked = jnp.stack([mom_fo, mom_ff, sum_oo, mom_ee])
    owned = lax.psum_scatter(stacked, DATE, scatter_dimension=2, tiled=True)
    total_dates = over_copies(count, DATE)
    samples = hindcast_portion * n_year * total_dates.astype(jnp.float32)
    acc = owned[0] / jnp.sqrt(owned[1] * owned[2] + 1e-06)
    rmse = jnp.sqrt(owned[3] / samples)
    quarter = owned.shape[2]
    start = (
        lax.axis_index("pix") * grid_points
        + (lax.axis_index(YEAR) * n_date + lax.axis_index(DATE)) * quarter
    )
    global_pixel = start + jnp.arange(quarter, dtype=jnp.int32)
    rows = (global_pixel % 181 - 90).astype(jnp.float32)
    lat_weight = jnp.cos(rows * (math.pi / 180.0))
    numer = jnp.stack([jnp.sum(acc * lat_weight, axis=1), jnp.sum(rmse * lat_weight, axis=1)])
    numer, weight_total = (
        one_axis_at_a_time(numer, YEAR_DATE_PIX),
        one_axis_at_a_time(jnp.sum(lat_weight), YEAR_DATE_PIX),
    )
    scores = numer / weight_total
    return (bias_share[None, :, None, :], acc[:, None, :], rmse[:, None, :], scores)


def solution(mesh):
    torus = Mesh(
        mesh.devices.reshape(4, 2, 2, 4, mesh.shape["pix"]),
        ("year_0", "year_1", "date_0", "date_1", "pix"),
    )
    return jax.shard_map(
        body,
        mesh=torus,
        in_specs=(P(YEAR, DATE, None, None, "pix"), P(YEAR, DATE, None, None, "pix"), P(DATE)),
        out_specs=(
            P(DATE, None, "pix", YEAR),
            P(None, "pix", YEAR_DATE),
            P(None, "pix", YEAR_DATE),
            P(),
        ),
        check_vma=False,
    )
```

profile of v0, /device:TPU:1, one launch (start us, length us, event | category | flops | bytes accessed | tf_op | source)
XLA Modules:
  0.0 298.1 jit_solution(10235149119093007746)
XLA Ops:
  7.2 0.0 reduce-scatter.3.cloned.1.call-start
  7.9 74.1 %fusion.3 = (f32[83,8192]{1,0:T(8,128)S(1)}, f32[83,8192]{1,0:T(8,128)S(1)}, f32[83,8192]{1,0:T(8,128)S(1)}, f32[83,8192]{1,0:T(8,128)S(1)}, f32[83,8192]{1,0:T(8,128)S(1)}) fusion(bf16[2,1,4,83,8192]{4,2,3,1,0:T(4,128)(2,1)} %param.4, f32[4]{0:T(128)S(1)} %compare_convert_fusion, bf16[2,1,4,83,8192]{4,2,3,1,0:T(4,128)(2,1)} %param.3), kind=kLoop, calls=%fused_computation.8 | loop fusion | flops 61874176 | bytes 35356688 | tf_op jit(solution)/shard_map/reduce_sum | solution.py:49
  82.0 1.8 bitcast_dynamic-update-slice_fusion.4
  83.8 1.8 bitcast_dynamic-update-slice_fusion.3
  85.6 1.8 bitcast_dynamic-update-slice_fusion.2
  87.4 1.9 bitcast_dynamic-update-slice_fusion.1
  89.3 1.9 bitcast_dynamic-update-slice_fusion
  91.2 0.0 reduce-scatter.3.cloned.1.call-update
  91.2 0.0 reduce-scatter.5.cloned.1.call-start
  91.3 83.8 %reduce-scatter.3.cloned.1.call-done = f32[5,83,1024]{2,1,0:T(8,128)} async-done(((f32[5,83,8192]{2,1,0:T(8,128)}), f32[5,83,1024]{2,1,0:T(8,128)}) %reduce-scatter.3.cloned.1.call-update) | async-done | bytes 1699856 | tf_op jit(solution)/shard_map/reduce_scatter | solution.py:52
  175.1 1.3 multiply_subtract_fusion
  176.4 1.6 subtract_add_fusion.1
  178.0 1.3 pad_maximum_fusion
  179.3 0.0 reduce-scatter.5.cloned.1.call-update
  179.3 0.6 broadcast_in_dim.2
  179.9 6.6 %all-to-all-start = ((s32[8,1,1]{2,1,0:T(1,128)}), s32[8,1,1]{2,1,0:T(1,128)S(1)}, u32[]{:S(2)}, u32[]{:S(2)}) async-start(s32[8,1,1]{2,1,0:T(1,128)} %broadcast_in_dim.2), calls=%async_computation.2 | async-start | bytes 8192 | tf_op jit(solution)/shard_map/all_to_all | solution.py:18
  186.5 0.7 fusion.14
  187.2 0.1 fusion.13
  187.3 5.7 %all-to-all-done = s32[8,1,1]{2,1,0:T(1,128)S(1)} async-done(((s32[8,1,1]{2,1,0:T(1,128)}), s32[8,1,1]{2,1,0:T(1,128)S(1)}, u32[]{:S(2)}, u32[]{:S(2)}) %all-to-all-start) | async-done | bytes 64 | tf_op jit(solution)/shard_map/all_to_all | solution.py:18
  192.9 0.6 reduce_sum.86
  194.2 1.0 reshape_bitcast_fusion
  195.2 57.0 %reduce-scatter.5.cloned.1.call-done = f32[4,83,128]{2,1,0:T(8,128)} async-done(((f32[4,83,1024]{2,1,0:T(8,128)}), f32[4,83,128]{2,1,0:T(8,128)}) %reduce-scatter.5.cloned.1.call-update) | async-done | bytes 170000 | tf_op jit(solution)/shard_map/reduce_scatter | solution.py:64
  252.2 0.8 fusion.4
  253.0 0.7 copy.24
  253.7 0.9 fusion.9
  254.6 0.7 div.51
  255.3 8.9 %all-reduce.1 = (f32[2,83]{1,0:T(2,128)S(1)}, f32[]{:T(128)}) all-reduce(f32[2,83]{1,0:T(2,128)S(1)} %pad_maximum_fusion.1, f32[]{:T(128)} %fusion.14), channel_id=1, replica_groups=mesh['year_0'=4,'year_1'=2,'date_0'=2,'date_1'=4,'pix'=2] {'year_0'}, use_global_device_ids=true, to_apply=%region_10.11 | all-reduce | flops 167 | bytes 1336 | tf_op jit(solution)/shard_map/psum | solution.py:26
  264.2 6.6 %all-reduce.4 = (f32[2,83]{1,0:T(2,128)S(1)}, f32[]{:T(128)}) all-reduce(f32[2,83]{1,0:T(2,128)S(1)} %get-tuple-element.25, f32[]{:T(128)} %get-tuple-element.26), channel_id=1, replica_groups=mesh['year_0'=4,'year_1'=2,'date_0'=2,'date_1'=4,'pix'=2] {'year_1'}, use_global_device_ids=true, to_apply=%region_11.12 | all-reduce | flops 167 | bytes 1336 | tf_op jit(solution)/shard_map/psum | solution.py:26
  270.8 5.9 %all-reduce.3 = (f32[2,83]{1,0:T(2,128)S(1)}, f32[]{:T(128)}) all-reduce(f32[2,83]{1,0:T(2,128)S(1)} %get-tuple-element.31, f32[]{:T(128)} %get-tuple-element.32), channel_id=1, replica_groups=mesh['year_0'=4,'year_1'=2,'date_0'=2,'date_1'=4,'pix'=2] {'date_0'}, use_global_device_ids=true, to_apply=%region_12.13 | all-reduce | flops 167 | bytes 1336 | tf_op jit(solution)/shard_map/psum | solution.py:26
  276.7 8.8 %all-reduce = (f32[2,83]{1,0:T(2,128)S(1)}, f32[]{:T(128)}) all-reduce(f32[2,83]{1,0:T(2,128)S(1)} %get-tuple-element.29, f32[]{:T(128)} %get-tuple-element.30), channel_id=1, replica_groups=mesh['year_0'=4,'year_1'=2,'date_0'=2,'date_1'=4,'pix'=2] {'date_1'}, use_global_device_ids=true, to_apply=%region_13.14 | all-reduce | flops 167 | bytes 1336 | tf_op jit(solution)/shard_map/psum | solution.py:26
  285.5 4.5 %all-reduce.2 = (f32[2,83]{1,0:T(2,128)S(1)}, f32[]{:T(128)}) all-reduce(f32[2,83]{1,0:T(2,128)S(1)} %get-tuple-element.23, f32[]{:T(128)} %get-tuple-element.24), channel_id=1, replica_groups=mesh['year_0'=4,'year_1'=2,'date_0'=2,'date_1'=4,'pix'=2] {'pix'}, use_global_device_ids=true, to_apply=%region_14.15 | all-reduce | flops 167 | bytes 1336 | tf_op jit(solution)/shard_map/psum | solution.py:26
  290.0 1.3 broadcast_divide_fusion.1
  (3 shorter events, 0.1 us)
Async XLA Ops:
  7.2 167.9 %reduce-scatter.3.cloned.1.call-start = ((), (), s32[]{:S(2)}) async-start(), calls=%async_computation.3 | async-start | bytes 16220160 | tf_op jit(solution)/shard_map/reduce_scatter | solution.py:52
  91.2 161.0 %reduce-scatter.5.cloned.1.call-start = ((), (), s32[]{:S(2)}) async-start(), calls=%async_computation.4 | async-start | bytes 1622016 | tf_op jit(solution)/shard_map/reduce_scatter | solution.py:64
  179.9 13.0 %all-to-all-start = ((s32[8,1,1]{2,1,0:T(1,128)}), s32[8,1,1]{2,1,0:T(1,128)S(1)}, u32[]{:S(2)}, u32[]{:S(2)}) async-start(s32[8,1,1]{2,1,0:T(1,128)} %broadcast_in_dim.2), calls=%async_computation.2 | async-start | bytes 8192 | tf_op jit(solution)/shard_map/all_to_all | solution.py:18
Sparse Core Ops, SparseCore 0:
  91.3 83.7 reduce-scatter.2
  179.4 72.6 reduce-scatter.4
where the time goes:
time: 302 us; the launch traced here: 298 us
  waiting for transfers between devices  147 us (49%)
  other arithmetic  82.8 us (27%)
  blocking collectives  34.7 us (11%)
  between operations  15.4 us (5%)
  local copies, waits for them, and re-layouts  12.1 us (4%)
  starting transfers between devices  6.65 us (2%)
    reduce_scatter x1, waiting for transfers between devices, body(): gathered_raw = lax.psum_scatter(raw, YEAR, scatter_dimension=2, tiled=True)  83.8 us
    reduce_sum x1, other arithmetic, body(): jnp.sum(omask * owide, axis=(0, 1))  74.1 us
    reduce_scatter x1, waiting for transfers between devices, body(): owned = lax.psum_scatter(stacked, DATE, scatter_dimension=2, tiled=True)  57 us
    psum x5, blocking collectives, one_axis_at_a_time(): return functools.reduce(lax.psum, axes, x)  34.7 us
    unnamed x7, local copies, waits for them, and re-layouts  8.97 us
    all_to_all x1, starting transfers between devices, copy_for_each(): return lax.all_to_all(copies, axis, split_axis=0, concat_axis=0, tiled=True)  6.57 us
  transfers between devices with their start and end apart: 3, of which 3 were waited for; matrix products, arithmetic and copies ran while one was open for 1% of the time, Pallas kernels for 0%

commit v1 on v0

v1 whole, which is shorter than its diff:
```python
import functools
import math

import jax
import jax.numpy as jnp
import numpy as np
from jax import lax
from jax.experimental import pallas as pl
from jax.experimental.pallas import tpu as pltpu
from jax.sharding import PartitionSpec as P

MESH = pl.DeviceIdType.MESH
F32 = jnp.float32
LANES = 128
TOTAL_COUNT = 20
E, T, OO, FF, EE = range(5)


def kernel(rows, years, dates, band, spans, weight_total, count_ref, f_hbm, o_hbm, bias_ref, acc_ref, rmse_ref, score_ref, *scratch):
    n_chunk = len(spans)
    per_chunk = 14
    bufs = [scratch[i * per_chunk:(i + 1) * per_chunk] for i in range(n_chunk)]
    (in_sem, send_sem, recv_sem, maps, mine, group_a, group_b, sa_sem, ra_sem, sb_sem, rb_sem) = scratch[n_chunk * per_chunk:]

    yr, dt, px = lax.axis_index("year"), lax.axis_index("date"), lax.axis_index("pix")
    x, c = yr // 2, yr % 2
    zh, y = dt // 4, dt % 4

    def device(dx=0, dc=0, dy=0, dz=0):
        return (((x + dx) % 4) * 2 + (c + dc) % 2, ((zh + dz) % 2) * 4 + (y + dy) % 4, px)

    loads = []
    for i, (first, high, _) in enumerate(spans):
        pair = []
        for which, (src, dst) in enumerate(((f_hbm, bufs[i][0]), (o_hbm, bufs[i][1]))):
            copy = pltpu.make_async_copy(
                src.at[:, 0, :, pl.ds(first, high), :], dst, in_sem.at[i, which])
            copy.start()
            pair.append(copy)
        loads.append(pair)

    barrier = pltpu.get_barrier_semaphore()
    for d in range(1, years):
        pl.semaphore_signal(barrier, inc=1, device_id=((yr + d) % years, dt, px), device_id_type=MESH)
    for d in range(1, 2 * dates):
        pl.semaphore_signal(
            barrier, inc=1, device_id=(yr, (dt + d // 2) % dates, (px + d % 2) % 2), device_id_type=MESH)

    maps[...] = jnp.zeros_like(maps)
    count = count_ref[0]
    weights = [(s < count).astype(F32) for s in range(4)]
    scale = 1.0 / (2 * years * count.astype(F32))

    sent = [[] for _ in range(n_chunk)]
    arriving = [{} for _ in range(n_chunk)]

    def send(i, name, src, dst, target):
        number = len(sent[i])
        copy = pltpu.make_async_remote_copy(
            src_ref=src, dst_ref=dst, send_sem=send_sem.at[i, number], recv_sem=recv_sem.at[i, number],
            device_id=target, device_id_type=MESH)
        copy.start()
        sent[i].append(copy)
        arriving[i].setdefault(name, []).append(copy)

    def arrive(i, name):
        for copy in arriving[i].pop(name):
            copy.wait_recv()

    def local_sums(i, n):
        fb, ob, w = bufs[i][0], bufs[i][1], bufs[i][2]
        height = spans[i][2]

        def step(km, carry):
            k, m = km // 2, km % 2
            base = ((((x + k) % 4) * 2 + (c + n) % 2) * 8 + ((zh + m) % 2) * 4) * LANES
            for j in range(4):
                lanes = pl.ds(pl.multiple_of(base + ((y + j) % 4) * LANES, LANES), LANES)
                totals = None
                for s in range(4):
                    vals = []
                    for year in range(2):
                        f = fb[year, s, :, lanes].astype(F32)[:height]
                        o = ob[year, s, :, lanes].astype(F32)[:height]
                        if s > 0:
                            f, o = f * weights[s], o * weights[s]
                        d = f - o
                        vals.append((f, o, f * f, o * o, d * d))
                    both = [a + b for a, b in zip(*vals)]
                    totals = both if totals is None else [a + b for a, b in zip(totals, both)]
                sf, so, ff, oo, ee = totals
                w[n, E, k, m, j] = sf - so
                w[n, T, k, m, j] = sf + so
                w[n, OO, k, m, j] = oo
                w[n, FF, k, m, j] = ff
                w[n, EE, k, m, j] = ee
            return carry

        lax.fori_loop(0, 8, step, 0)

    def stage0(i):
        w, dr = bufs[i][2], bufs[i][3]
        for copy in loads[i]:
            copy.wait()
        local_sums(i, 1)
        if i == 0:
            pl.semaphore_wait(barrier, years - 1 + 2 * dates - 1)
        send(i, "core", w.at[1], dr, device(dc=1))
        local_sums(i, 0)

    def stage1(i):
        (_, _, w, dr, x1, x2, y1e, y2e, ze, za, y1a, y2a, xq, late) = bufs[i]
        arrive(i, "core")

        def add(qk, carry):
            q, k = qk // 4, qk % 4
            w[0, q, k] = w[0, q, k] + dr[q, k]
            return carry

        lax.fori_loop(0, 20, add, 0)
        for h, way in enumerate((1, 3)):
            send(i, "x1", w.at[0, 0:2, 2, h], x1.at[h], device(dx=way))
        for h, way in enumerate((1, 3)):
            send(i, "y1e", w.at[0, 3:5, 1:4, h, 2], y1e.at[h], device(dy=way))
        send(i, "za", w.at[0, OO, :, 1], za, device(dz=1))

    def stage2(i):
        (_, _, w, dr, x1, x2, y1e, y2e, ze, za, y1a, y2a, xq, late) = bufs[i]
        arrive(i, "x1")
        w[0, 0:2, 1, 0] = w[0, 0:2, 1, 0] + x1[0]
        w[0, 0:2, 3, 1] = w[0, 0:2, 3, 1] + x1[1]
        send(i, "x2", w.at[0, 0:2, 1], x2.at[0], device(dx=1))
        send(i, "x2", w.at[0, 0:2, 3], x2.at[1], device(dx=3))
        arrive(i, "y1e")
        w[0, 3:5, 1:4, 0, 1] = w[0, 3:5, 1:4, 0, 1] + y1e[0]
        w[0, 3:5, 1:4, 1, 3] = w[0, 3:5, 1:4, 1, 3] + y1e[1]
        send(i, "y2e", w.at[0, 3:5, 1:4, :, 1], y2e.at[0], device(dy=1))
        send(i, "y2e", w.at[0, 3:5, 1:4, :, 3], y2e.at[1], device(dy=3))
        arrive(i, "za")
        w[0, OO, :, 0] = w[0, OO, :, 0] + za[...]
        for h, way in enumerate((1, 3)):
            send(i, "y1a", w.at[0, OO, 2 * h:2 * h + 2, 0, 2], y1a.at[h], device(dy=way))

    def stage3(i):
        (_, _, w, dr, x1, x2, y1e, y2e, ze, za, y1a, y2a, xq, late) = bufs[i]
        first, high, height = spans[i]
        arrive(i, "x2")
        for m in range(2):
            for j in range(4):
                e = w[0, E, 0, m, j] + x2[0, E, m, j] + x2[1, E, m, j]
                t = w[0, T, 0, m, j] + x2[0, T, m, j] + x2[1, T, m, j]
                b = e * scale
                lanes = pl.ds(pl.multiple_of((((zh + m) % 2) * 4 + (y + j) % 4) * LANES, LANES), LANES)
                bias_ref[pl.ds(first, high), lanes] = b[:high]
                w[0, FF, 0, m, j] = w[0, FF, 0, m, j] - b * t
                w[0, EE, 0, m, j] = w[0, EE, 0, m, j] - b * e
        for h, way in enumerate((1, 3)):
            send(i, "y1l", w.at[0, 3:5, 0, h, 2], late.at[0, h], device(dy=way))
        arrive(i, "y2e")
        for m in range(2):
            w[0, 3:5, 1:4, m, 0] = w[0, 3:5, 1:4, m, 0] + y2e[0, :, :, m] + y2e[1, :, :, m]
        send(i, "ze", w.at[0, 3:5, 1:4, 1, 0], ze, device(dz=1))
        arrive(i, "y1a")
        w[0, OO, 0:2, 0, 1] = w[0, OO, 0:2, 0, 1] + y1a[0]
        w[0, OO, 2:4, 0, 3] = w[0, OO, 2:4, 0, 3] + y1a[1]
        send(i, "y2a", w.at[0, OO, :, 0, 1], y2a.at[0], device(dy=1))
        send(i, "y2a", w.at[0, OO, :, 0, 3], y2a.at[1], device(dy=3))

    def stage4(i):
        (_, _, w, dr, x1, x2, y1e, y2e, ze, za, y1a, y2a, xq, late) = bufs[i]
        arrive(i, "ze")
        w[0, 3:5, 1:4, 0, 0] = w[0, 3:5, 1:4, 0, 0] + ze[...]
        arrive(i, "y2a")
        w[0, OO, :, 0, 0] = w[0, OO, :, 0, 0] + y2a[0] + y2a[1]
        for k in range(1, 4):
            send(i, "xq", w.at[0, 2:5, k, 0, 0], xq.at[k - 1], device(dx=k))
        arrive(i, "y1l")
        w[0, 3:5, 0, 0, 1] = w[0, 3:5, 0, 0, 1] + late[0, 0]
        w[0, 3:5, 0, 1, 3] = w[0, 3:5, 0, 1, 3] + late[0, 1]
        send(i, "y2l", w.at[0, 3:5, 0, :, 1], late.at[1], device(dy=1))
        send(i, "y2l", w.at[0, 3:5, 0, :, 3], late.at[2], device(dy=3))

    def stage5(i):
        w, late = bufs[i][2], bufs[i][13]
        arrive(i, "y2l")
        for m in range(2):
            w[0, 3:5, 0, m, 0] = w[0, 3:5, 0, m, 0] + late[1, :, m] + late[2, :, m]
        send(i, "zl", w.at[0, 3:5, 0, 1, 0], late.at[3, 0], device(dz=1))

    def stage6(i):
        w, xq, late = bufs[i][2], bufs[i][12], bufs[i][13]
        first, high, height = spans[i]
        arrive(i, "zl")
        arrive(i, "xq")
        oo, ff, ee = [w[0, q, 0, 0, 0] + xq[0, q - 2] + xq[1, q - 2] + xq[2, q - 2] for q in (OO, FF, EE)]
        ff = ff + late[3, 0, 0]
        ee = ee + late[3, 0, 1]
        fo = 0.5 * (ff + oo - ee)
        acc = fo / jnp.sqrt(ff * oo + 1e-06)
        rmse = jnp.sqrt(jnp.maximum(ee, 0.0) / (2.0 * years * TOTAL_COUNT))
        acc_ref[pl.ds(first, high), :] = acc[:high]
        rmse_ref[pl.ds(first, high), :] = rmse[:high]
        maps[0, pl.ds(first, height), :] = acc
        maps[1, pl.ds(first, height), :] = rmse

    stages = (stage0, stage1, stage2, stage3, stage4, stage5, stage6)
    for turn in range(n_chunk + len(stages) - 1):
        for s in reversed(range(len(stages))):
            if 0 <= turn - s < n_chunk:
                stages[s](turn - s)

    pixel = px * band + (yr * dates + dt) * LANES + lax.broadcasted_iota(jnp.int32, (8, LANES), 1)
    lat = jnp.cos((pixel % 181 - 90).astype(F32) * (math.pi / 180.0))
    sums = [
        lax.dot_general(lat, maps[which], (((1,), (1,)), ((), ())), precision=lax.Precision.HIGHEST,
                        preferred_element_type=F32)
        for which in range(2)
    ]
    is_acc = lax.broadcasted_iota(jnp.int32, sums[0].shape, 0) == 0
    mine[...] = jnp.zeros_like(mine)
    mine[:, 0:sums[0].shape[1]] = jnp.where(is_acc, sums[0], sums[1])

    def exchange(own, group, ssem, rsem, me, n, target):
        copies = []
        for d in range(1, n):
            copy = pltpu.make_async_remote_copy(
                src_ref=own, dst_ref=group.at[me], send_sem=ssem.at[d], recv_sem=rsem.at[me],
                device_id=target(d), device_id_type=MESH)
            copy.start()
            copies.append(copy)
        group[me] = own[...]
        for d in range(1, n):
            other = (me + d) % n
            pltpu.make_async_remote_copy(
                src_ref=own, dst_ref=group.at[other], send_sem=ssem.at[d], recv_sem=rsem.at[other],
                device_id=target(d), device_id_type=MESH).wait_recv()
        for copy in copies:
            copy.wait_send()
        total = group[0]
        for d in range(1, n):
            total = total + group[d]
        return total

    own_sum = exchange(mine.at[0:8], group_a, sa_sem, ra_sem, yr, years, lambda d: ((yr + d) % years, dt, px))
    mine[...] = own_sum
    place = dt * 2 + px

    def in_group_b(d):
        other = (place + d) % (2 * dates)
        return (yr, other // 2, other % 2)

    total = exchange(mine.at[0:8], group_b, sb_sem, rb_sem, place, 2 * dates, in_group_b)
    score_ref[...] = total[0:2, 0:rows] * (1.0 / weight_total)
    for i in range(n_chunk):
        for copy in sent[i]:
            copy.wait_send()


def solution(mesh):
    years, dates = mesh.shape["year"], mesh.shape["date"]

    def body(predicted_anomaly, measured_anomaly, filled_calendar):
        _, _, slots, rows, band = predicted_anomaly.shape
        grid = band * mesh.shape["pix"]
        weight_total = float(np.sum(np.cos((np.arange(grid) % 181 - 90) * (math.pi / 180.0))))
        spans = []
        for first in range(0, rows, 16):
            high = min(16, rows - first)
            spans.append((first, high, high))
        scratch = []
        for _, rows_in, h in spans:
            def vm(*shape):
                return pltpu.VMEM((*shape, h, LANES), F32)
            scratch += [
                pltpu.VMEM((2, slots, rows_in, band), jnp.bfloat16),
                pltpu.VMEM((2, slots, rows_in, band), jnp.bfloat16),
                vm(2, 5, 4, 2, 4),
                vm(5, 4, 2, 4),
                vm(2, 2, 4),
                vm(2, 2, 2, 4),
                vm(2, 2, 3),
                vm(2, 2, 3, 2),
                vm(2, 3),
                vm(4, 4),
                vm(2, 2),
                vm(2, 4),
                vm(3, 3),
                vm(4, 2, 2),
            ]
        n_chunk = len(spans)
        tall = -(-rows // 8) * 8
        scratch += [
            pltpu.SemaphoreType.DMA((n_chunk, 2)),
            pltpu.SemaphoreType.DMA((n_chunk, 23)),
            pltpu.SemaphoreType.DMA((n_chunk, 23)),
            pltpu.VMEM((2, tall, LANES), F32),
            pltpu.VMEM((8, LANES), F32),
            pltpu.VMEM((years, 8, LANES), F32),
            pltpu.VMEM((2 * dates, 8, LANES), F32),
            pltpu.SemaphoreType.DMA((years,)),
            pltpu.SemaphoreType.DMA((years,)),
            pltpu.SemaphoreType.DMA((2 * dates,)),
            pltpu.SemaphoreType.DMA((2 * dates,)),
        ]
        bias, acc, rmse, scores = pl.pallas_call(
            functools.partial(kernel, rows, years, dates, band, spans, weight_total),
            name="bias_and_maps",
            out_shape=(
                jax.ShapeDtypeStruct((rows, band // years), F32),
                jax.ShapeDtypeStruct((rows, LANES), F32),
                jax.ShapeDtypeStruct((rows, LANES), F32),
                jax.ShapeDtypeStruct((2, rows), F32),
            ),
            in_specs=[
                pl.BlockSpec(memory_space=pltpu.SMEM),
                pl.BlockSpec(memory_space=pl.ANY),
                pl.BlockSpec(memory_space=pl.ANY),
            ],
            out_specs=[pl.BlockSpec(memory_space=pltpu.VMEM)] * 4,
            scratch_shapes=scratch,
            compiler_params=pltpu.CompilerParams(
                collective_id=0, has_side_effects=True, vmem_limit_bytes=60 * 2**20),
        )(filled_calendar, predicted_anomaly, measured_anomaly)
        return bias[None, :, None, :], acc[:, None, :], rmse[:, None, :], scores

    return jax.shard_map(
        body,
        mesh=mesh,
        in_specs=(P("year", "date", None, None, "pix"), P("year", "date", None, None, "pix"), P("date")),
        out_specs=(
            P("date", None, "pix", "year"),
            P(None, "pix", ("year", "date")),
            P(None, "pix", ("year", "date")),
            P(),
        ),
        check_vma=False,
    )
```

time: 302 us -> 103 us (0.34); the launches traced: 298 us -> 102 us
  waiting for transfers between devices: 147 us -> 0 us
  other arithmetic: 82.8 us -> 0.01 us
  Pallas kernels: 0 us -> 74 us
  blocking collectives: 34.7 us -> 0 us
  local copies, waits for them, and re-layouts: 12.1 us -> 26.9 us
  between operations: 15.4 us -> 1.47 us
  starting transfers between devices: 6.65 us -> 0 us
    reduce_scatter x2 -> x0, waiting for transfers between devices: 141 us -> none  [the longest x1 83.8 us: body(): gathered_raw = lax.psum_scatter(raw, YEAR, scatter_dimension=2, tiled=True)]
    reduce_sum x4 -> x0, other arithmetic: 76.4 us -> none  [the longest x1 74.1 us: body(): jnp.sum(omask * owide, axis=(0, 1))]
    pallas_call x0 -> x1, Pallas kernels: none -> 74 us  [body(): pl.pallas_call(functools.partial(kernel, rows, years, dates, band, spans,...]
    psum x5 -> x0, blocking collectives: 34.7 us -> none  [one_axis_at_a_time(): return functools.reduce(lax.psum, axes, x)]
    unnamed x7 -> x12, local copies, waits for them, and re-layouts: 8.97 us -> 26.9 us
    all_to_all x1 -> x0, starting transfers between devices: 6.57 us -> none  [copy_for_each(): return lax.all_to_all(copies, axis, split_axis=0, concat_axis=0, tiled=True)]
    all_to_all x1 -> x0, waiting for transfers between devices: 5.66 us -> none  [copy_for_each(): return lax.all_to_all(copies, axis, split_axis=0, concat_axis=0, tiled=True)]
  transfers between devices with their start and end apart: 3 -> 0, of which waited for: 3 -> 0; matrix products, arithmetic and copies ran while one was open for 1% -> 0% of each run, Pallas kernels for 0% -> 0%
where the time goes in v1:
time: 103 us; the launch traced here: 102 us
  Pallas kernels  74 us (72%)
  local copies, waits for them, and re-layouts  26.9 us (26%)
  between operations  1.47 us (1%)
    pallas_call x1, Pallas kernels, body(): pl.pallas_call(functools.partial(kernel, rows, years, dates, band, spans,...  74 us
    unnamed x12, local copies, waits for them, and re-layouts  26.9 us

profile of v1, /device:TPU:1, one launch (start us, length us, event | category | flops | bytes accessed | tf_op | source)
XLA Modules:
  0.0 102.4 jit_solution(17634276619263991730)
XLA Ops:
  0.6 0.0 slice-start
  1.4 0.0 slice-start.1
  1.4 0.0 slice-start.2
  1.5 12.3 %copy.7.f_hbm = bf16[2,1,4,83,8192]{4,3,2,1,0:T(8,128)(2,1)} copy(bf16[2,1,4,83,8192]{4,2,3,1,0:T(4,128)(2,1)} %param.3) | data formatting | bytes 21757952 | tf_op args[0]
  13.8 0.0 slice-done
  13.8 0.0 slice-done.1
  13.8 0.0 slice-done.2
  13.8 8.4 %copy.8.o_hbm = bf16[2,1,4,83,8192]{4,3,2,1,0:T(8,128)(2,1)} copy(bf16[2,1,4,83,8192]{4,2,3,1,0:T(4,128)(2,1)S(1)} %bitcast.4) | data formatting | bytes 21757952 | tf_op args[1]
  22.2 74.0 %bias_and_maps.1 = (f32[83,1024]{1,0:T(8,128)}, f32[83,128]{1,0:T(8,128)}, f32[83,128]{1,0:T(8,128)}, f32[2,83]{1,0:T(2,128)}) custom-call(s32[1]{0:T(128)S(6)} %copy.13.count_ref, bf16[2,1,4,83,8192]{4,3,2,1,0:T(8,128)(2,1)} %copy.7.f_hbm, bf16[2,1,4,83,8192]{4,3,2,1,0:T(8,128)(2,1)} %copy.8.o_hbm), custom_call_target="tpu_custom_call" | custom-call | tf_op jit(solution)/shard_map/bias_and_maps/pallas_call | solution.py:305
  96.2 2.1 %copy.9 = f32[1,83,1,1024]{3,2,1,0:T(1,128)} copy(f32[1,83,1,1024]{3,1,2,0:T(8,128)} %bitcast.5) | data formatting | bytes 679936
  98.2 1.4 %copy.10 = f32[83,1,128]{2,1,0:T(1,128)} copy(f32[83,1,128]{2,0,1:T(8,128)} %bitcast.7) | data formatting | bytes 84992
  99.7 1.4 %copy.11 = f32[83,1,128]{2,1,0:T(1,128)} copy(f32[83,1,128]{2,0,1:T(8,128)} %bitcast.6) | data formatting | bytes 84992
  101.1 1.2 %copy.14 = f32[2,83]{1,0:T(2,128)} copy(f32[2,83]{1,0:T(2,128)} %get-tuple-element.23) | data formatting | bytes 1328
  (1 shorter events, 0.0 us)
Async XLA Ops:
  0.6 13.2 %slice-start = ((s8[10878976]{0:T(1024)(128)(4,1)}), s8[4194304]{0:T(1024)(128)(4,1)S(1)}, s32[]{:S(2)}) async-start(s8[10878976]{0:T(1024)(128)(4,1)} %bitcast.3), calls=%async_computation | async-start | bytes 8388608
  1.4 12.4 %slice-start.1 = ((s8[10878976]{0:T(1024)(128)(4,1)}), s8[4194304]{0:T(1024)(128)(4,1)S(1)}, s32[]{:S(2)}) async-start(s8[10878976]{0:T(1024)(128)(4,1)} %bitcast.3), calls=%async_computation.1 | async-start | bytes 8388608
  1.4 12.4 %slice-start.2 = ((s8[10878976]{0:T(1024)(128)(4,1)}), s8[2490368]{0:T(1024)(128)(4,1)S(1)}, s32[]{:S(2)}) async-start(s8[10878976]{0:T(1024)(128)(4,1)} %bitcast.3), calls=%async_computation.2 | async-start | bytes 4980736

commit v2 on v1

--- a/solution.py
+++ b/solution.py
@@ -20,7 +20,7 @@
     n_chunk = len(spans)
     per_chunk = 14
     bufs = [scratch[i * per_chunk:(i + 1) * per_chunk] for i in range(n_chunk)]
-    (in_sem, send_sem, recv_sem, maps, mine, group_a, group_b, sa_sem, ra_sem, sb_sem, rb_sem) = scratch[n_chunk * per_chunk:]
+    (in_sem, wide, send_sem, recv_sem, maps, mine, group_a, group_b, sa_sem, ra_sem, sb_sem, rb_sem) = scratch[n_chunk * per_chunk:]
 
     yr, dt, px = lax.axis_index("year"), lax.axis_index("date"), lax.axis_index("pix")
     x, c = yr // 2, yr % 2
@@ -29,15 +29,30 @@
     def device(dx=0, dc=0, dy=0, dz=0):
         return (((x + dx) % 4) * 2 + (c + dc) % 2, ((zh + dz) % 2) * 4 + (y + dy) % 4, px)
 
-    loads = []
-    for i, (first, high, _) in enumerate(spans):
-        pair = []
-        for which, (src, dst) in enumerate(((f_hbm, bufs[i][0]), (o_hbm, bufs[i][1]))):
-            copy = pltpu.make_async_copy(
-                src.at[:, 0, :, pl.ds(first, high), :], dst, in_sem.at[i, which])
-            copy.start()
-            pair.append(copy)
-        loads.append(pair)
+    slots = 4
+
+    def load(i, which):
+        first, high, _ = spans[i]
+        src, dst = (f_hbm, o_hbm)[which], bufs[i][which]
+
+        def start(channel, carry):
+            pltpu.make_async_copy(
+                src.at[:, 0, first + channel],
+                dst.at[:, pl.ds(pl.multiple_of(channel * slots, slots), slots), :],
+                in_sem.at[i, which]).start()
+            return carry
+
+        lax.fori_loop(0, high, start, 0)
+
+    for i in range(n_chunk):
+        load(i, 0)
+        load(i, 1)
+
+    def loaded(i):
+        first, high, _ = spans[i]
+        for which, src in enumerate((f_hbm, o_hbm)):
+            part = src.at[:, 0, pl.ds(first, high)]
+            pltpu.make_async_copy(part, part, in_sem.at[i, which]).wait()
 
     barrier = pltpu.get_barrier_semaphore()
     for d in range(1, years):
@@ -70,18 +85,22 @@
     def local_sums(i, n):
         fb, ob, w = bufs[i][0], bufs[i][1], bufs[i][2]
         height = spans[i][2]
+        deep = fb.shape[1]
 
         def step(km, carry):
             k, m = km // 2, km % 2
             base = ((((x + k) % 4) * 2 + (c + n) % 2) * 8 + ((zh + m) % 2) * 4) * LANES
             for j in range(4):
                 lanes = pl.ds(pl.multiple_of(base + ((y + j) % 4) * LANES, LANES), LANES)
+                for year in range(2):
+                    wide[j, 0, year, 0:deep] = fb[year, :, lanes].astype(F32)
+                    wide[j, 1, year, 0:deep] = ob[year, :, lanes].astype(F32)
                 totals = None
-                for s in range(4):
+                for s in range(slots):
                     vals = []
                     for year in range(2):
-                        f = fb[year, s, :, lanes].astype(F32)[:height]
-                        o = ob[year, s, :, lanes].astype(F32)[:height]
+                        f = wide[j, 0, year, pl.ds(s, height, stride=slots), :]
+                        o = wide[j, 1, year, pl.ds(s, height, stride=slots), :]
                         if s > 0:
                             f, o = f * weights[s], o * weights[s]
                         d = f - o
@@ -100,8 +119,7 @@
 
     def stage0(i):
         w, dr = bufs[i][2], bufs[i][3]
-        for copy in loads[i]:
-            copy.wait()
+        loaded(i)
         local_sums(i, 1)
         if i == 0:
             pl.semaphore_wait(barrier, years - 1 + 2 * dates - 1)
@@ -205,7 +223,7 @@
 
     stages = (stage0, stage1, stage2, stage3, stage4, stage5, stage6)
     for turn in range(n_chunk + len(stages) - 1):
-        for s in reversed(range(len(stages))):
+        for s in (1, 0, 2, 3, 4, 5, 6):
             if 0 <= turn - s < n_chunk:
                 stages[s](turn - s)
 
@@ -272,8 +290,8 @@
             def vm(*shape):
                 return pltpu.VMEM((*shape, h, LANES), F32)
             scratch += [
-                pltpu.VMEM((2, slots, rows_in, band), jnp.bfloat16),
-                pltpu.VMEM((2, slots, rows_in, band), jnp.bfloat16),
+                pltpu.VMEM((2, -(-slots * rows_in // 16) * 16, band), jnp.bfloat16),
+                pltpu.VMEM((2, -(-slots * rows_in // 16) * 16, band), jnp.bfloat16),
                 vm(2, 5, 4, 2, 4),
                 vm(5, 4, 2, 4),
                 vm(2, 2, 4),
@@ -291,6 +309,7 @@
         tall = -(-rows // 8) * 8
         scratch += [
             pltpu.SemaphoreType.DMA((n_chunk, 2)),
+            pltpu.VMEM((4, 2, 2, slots * 16, LANES), F32),
             pltpu.SemaphoreType.DMA((n_chunk, 23)),
             pltpu.SemaphoreType.DMA((n_chunk, 23)),
             pltpu.VMEM((2, tall, LANES), F32),
@@ -320,7 +339,7 @@
             scratch_shapes=scratch,
             compiler_params=pltpu.CompilerParams(
                 collective_id=0, has_side_effects=True, vmem_limit_bytes=60 * 2**20),
-        )(filled_calendar, predicted_anomaly, measured_anomaly)
+        )(filled_calendar, jnp.transpose(predicted_anomaly, (0, 1, 3, 2, 4)), jnp.transpose(measured_anomaly, (0, 1, 3, 2, 4)))
         return bias[None, :, None, :], acc[:, None, :], rmse[:, None, :], scores
 
     return jax.shard_map(

time: 103 us -> 77.3 us (0.75)
  local copies, waits for them, and re-layouts: 26.9 us -> 6.2 us
  Pallas kernels: 74 us -> 69.6 us
    unnamed x12 -> x4, local copies, waits for them, and re-layouts: 26.9 us -> 6.2 us
    pallas_call x1, Pallas kernels: 74 us -> 69.6 us  [body(): pl.pallas_call(functools.partial(kernel, rows, years, dates, band, spans,...]
where the time goes in v2:
time: 77.3 us; the launch traced here: 77.1 us
  Pallas kernels  69.6 us (90%)
  local copies, waits for them, and re-layouts  6.2 us (8%)
  between operations  1.29 us (2%)
    pallas_call x1, Pallas kernels, body(): pl.pallas_call(functools.partial(kernel, rows, years, dates, band, spans,...  69.6 us
    unnamed x4, local copies, waits for them, and re-layouts  6.2 us

profile of v2, /device:TPU:1, one launch (start us, length us, event | category | flops | bytes accessed | tf_op | source)
XLA Modules:
  0.0 77.1 jit_solution(16879382592545727288)
XLA Ops:
  1.3 69.6 %bias_and_maps.1 = (f32[83,1024]{1,0:T(8,128)}, f32[83,128]{1,0:T(8,128)}, f32[83,128]{1,0:T(8,128)}, f32[2,83]{1,0:T(2,128)}) custom-call(s32[1]{0:T(128)S(6)} %copy.11.count_ref, bf16[2,1,83,4,8192]{4,3,2,1,0:T(4,128)(2,1)} %bitcast.5, bf16[2,1,83,4,8192]{4,3,2,1,0:T(4,128)(2,1)} %bitcast.6), custom_call_target="tpu_custom_call" | custom-call | tf_op jit(solution)/shard_map/bias_and_maps/pallas_call | solution.py:324
  70.9 2.1 %copy.7 = f32[1,83,1,1024]{3,2,1,0:T(1,128)} copy(f32[1,83,1,1024]{3,1,2,0:T(8,128)} %bitcast.7) | data formatting | bytes 679936
  72.9 1.4 %copy.8 = f32[83,1,128]{2,1,0:T(1,128)} copy(f32[83,1,128]{2,0,1:T(8,128)} %bitcast.9) | data formatting | bytes 84992
  74.4 1.4 %copy.9 = f32[83,1,128]{2,1,0:T(1,128)} copy(f32[83,1,128]{2,0,1:T(8,128)} %bitcast.8) | data formatting | bytes 84992
  75.8 1.2 %copy.12 = f32[2,83]{1,0:T(2,128)} copy(f32[2,83]{1,0:T(2,128)} %get-tuple-element.23) | data formatting | bytes 1328

commit v3 on v2

--- a/solution.py
+++ b/solution.py
@@ -20,7 +20,7 @@
     n_chunk = len(spans)
     per_chunk = 14
     bufs = [scratch[i * per_chunk:(i + 1) * per_chunk] for i in range(n_chunk)]
-    (in_sem, wide, send_sem, recv_sem, maps, mine, group_a, group_b, sa_sem, ra_sem, sb_sem, rb_sem) = scratch[n_chunk * per_chunk:]
+    (in_sem, wide, lat_ref, send_sem, recv_sem, maps, mine, group_a, group_b, sa_sem, ra_sem, sb_sem, rb_sem) = scratch[n_chunk * per_chunk:]
 
     yr, dt, px = lax.axis_index("year"), lax.axis_index("date"), lax.axis_index("pix")
     x, c = yr // 2, yr % 2
@@ -28,6 +28,13 @@
 
     def device(dx=0, dc=0, dy=0, dz=0):
         return (((x + dx) % 4) * 2 + (c + dc) % 2, ((zh + dz) % 2) * 4 + (y + dy) % 4, px)
+
+    barrier = pltpu.get_barrier_semaphore()
+    for d in range(1, years):
+        pl.semaphore_signal(barrier, inc=1, device_id=((yr + d) % years, dt, px), device_id_type=MESH)
+    for d in range(1, 2 * dates):
+        pl.semaphore_signal(
+            barrier, inc=1, device_id=(yr, (dt + d // 2) % dates, (px + d % 2) % 2), device_id_type=MESH)
 
     slots = 4
 
@@ -44,9 +51,8 @@
 
         lax.fori_loop(0, high, start, 0)
 
-    for i in range(n_chunk):
-        load(i, 0)
-        load(i, 1)
+    load(0, 0)
+    load(0, 1)
 
     def loaded(i):
         first, high, _ = spans[i]
@@ -54,14 +60,12 @@
             part = src.at[:, 0, pl.ds(first, high)]
             pltpu.make_async_copy(part, part, in_sem.at[i, which]).wait()
 
-    barrier = pltpu.get_barrier_semaphore()
-    for d in range(1, years):
-        pl.semaphore_signal(barrier, inc=1, device_id=((yr + d) % years, dt, px), device_id_type=MESH)
-    for d in range(1, 2 * dates):
-        pl.semaphore_signal(
-            barrier, inc=1, device_id=(yr, (dt + d // 2) % dates, (px + d % 2) % 2), device_id_type=MESH)
-
+    for i in range(1, min(2, n_chunk)):
+        load(i, 0)
+        load(i, 1)
     maps[...] = jnp.zeros_like(maps)
+    pixel = px * band + (yr * dates + dt) * LANES + lax.broadcasted_iota(jnp.int32, (8, LANES), 1)
+    lat_ref[...] = jnp.cos((pixel % 181 - 90).astype(F32) * (math.pi / 180.0))
     count = count_ref[0]
     weights = [(s < count).astype(F32) for s in range(4)]
     scale = 1.0 / (2 * years * count.astype(F32))
@@ -124,6 +128,11 @@
         if i == 0:
             pl.semaphore_wait(barrier, years - 1 + 2 * dates - 1)
         send(i, "core", w.at[1], dr, device(dc=1))
+        if i + 2 < n_chunk:
+            load(i + 2, 0)
+            load(i + 2, 1)
+
+    def stage0b(i):
         local_sums(i, 0)
 
     def stage1(i):
@@ -172,8 +181,8 @@
                 bias_ref[pl.ds(first, high), lanes] = b[:high]
                 w[0, FF, 0, m, j] = w[0, FF, 0, m, j] - b * t
                 w[0, EE, 0, m, j] = w[0, EE, 0, m, j] - b * e
-        for h, way in enumerate((1, 3)):
-            send(i, "y1l", w.at[0, 3:5, 0, h, 2], late.at[0, h], device(dy=way))
+        for r in range(1, 8):
+            send(i, "late", w.at[0, 3:5, 0, r // 4, r % 4], late.at[r - 1], device(dy=r % 4, dz=r // 4))
         arrive(i, "y2e")
         for m in range(2):
             w[0, 3:5, 1:4, m, 0] = w[0, 3:5, 1:4, m, 0] + y2e[0, :, :, m] + y2e[1, :, :, m]
@@ -192,27 +201,16 @@
         w[0, OO, :, 0, 0] = w[0, OO, :, 0, 0] + y2a[0] + y2a[1]
         for k in range(1, 4):
             send(i, "xq", w.at[0, 2:5, k, 0, 0], xq.at[k - 1], device(dx=k))
-        arrive(i, "y1l")
-        w[0, 3:5, 0, 0, 1] = w[0, 3:5, 0, 0, 1] + late[0, 0]
-        w[0, 3:5, 0, 1, 3] = w[0, 3:5, 0, 1, 3] + late[0, 1]
-        send(i, "y2l", w.at[0, 3:5, 0, :, 1], late.at[1], device(dy=1))
-        send(i, "y2l", w.at[0, 3:5, 0, :, 3], late.at[2], device(dy=3))
 
     def stage5(i):
-        w, late = bufs[i][2], bufs[i][13]
-        arrive(i, "y2l")
-        for m in range(2):
-            w[0, 3:5, 0, m, 0] = w[0, 3:5, 0, m, 0] + late[1, :, m] + late[2, :, m]
-        send(i, "zl", w.at[0, 3:5, 0, 1, 0], late.at[3, 0], device(dz=1))
-
-    def stage6(i):
         w, xq, late = bufs[i][2], bufs[i][12], bufs[i][13]
         first, high, height = spans[i]
-        arrive(i, "zl")
+        arrive(i, "late")
         arrive(i, "xq")
         oo, ff, ee = [w[0, q, 0, 0, 0] + xq[0, q - 2] + xq[1, q - 2] + xq[2, q - 2] for q in (OO, FF, EE)]
-        ff = ff + late[3, 0, 0]
-        ee = ee + late[3, 0, 1]
+        for r in range(7):
+            ff = ff + late[r, 0]
+            ee = ee + late[r, 1]
         fo = 0.5 * (ff + oo - ee)
         acc = fo / jnp.sqrt(ff * oo + 1e-06)
         rmse = jnp.sqrt(jnp.maximum(ee, 0.0) / (2.0 * years * TOTAL_COUNT))
@@ -221,14 +219,13 @@
         maps[0, pl.ds(first, height), :] = acc
         maps[1, pl.ds(first, height), :] = rmse
 
-    stages = (stage0, stage1, stage2, stage3, stage4, stage5, stage6)
-    for turn in range(n_chunk + len(stages) - 1):
-        for s in (1, 0, 2, 3, 4, 5, 6):
-            if 0 <= turn - s < n_chunk:
-                stages[s](turn - s)
-
-    pixel = px * band + (yr * dates + dt) * LANES + lax.broadcasted_iota(jnp.int32, (8, LANES), 1)
-    lat = jnp.cos((pixel % 181 - 90).astype(F32) * (math.pi / 180.0))
+    order = ((stage0, 0), (stage1, 1), (stage0b, 0), (stage2, 2), (stage3, 3), (stage4, 4), (stage5, 5))
+    for turn in range(n_chunk + max(lag for _, lag in order)):
+        for stage, lag in order:
+            if 0 <= turn - lag < n_chunk:
+                stage(turn - lag)
+
+    lat = lat_ref[...]
     sums = [
         lax.dot_general(lat, maps[which], (((1,), (1,)), ((), ())), precision=lax.Precision.HIGHEST,
                         preferred_element_type=F32)
@@ -274,6 +271,19 @@
             copy.wait_send()
 
 
+def place(bias, acc, rmse, score, bias_out, acc_out, rmse_out, score_out, sem):
+    copies = [
+        pltpu.make_async_copy(bias, bias_out.at[:, 0, :], sem.at[0]),
+        pltpu.make_async_copy(acc, acc_out.at[:, 0, :], sem.at[1]),
+        pltpu.make_async_copy(rmse, rmse_out.at[:, 0, :], sem.at[2]),
+        pltpu.make_async_copy(score, score_out, sem.at[3]),
+    ]
+    for copy in copies:
+        copy.start()
+    for copy in copies:
+        copy.wait()
+
+
 def solution(mesh):
     years, dates = mesh.shape["year"], mesh.shape["date"]
 
@@ -281,10 +291,11 @@
         _, _, slots, rows, band = predicted_anomaly.shape
         grid = band * mesh.shape["pix"]
         weight_total = float(np.sum(np.cos((np.arange(grid) % 181 - 90) * (math.pi / 180.0))))
-        spans = []
-        for first in range(0, rows, 16):
-            high = min(16, rows - first)
+        spans, first = [], 0
+        for high in (8, 16, 16, 16, 16, 11):
             spans.append((first, high, high))
+            first += high
+        assert first == rows
         scratch = []
         for _, rows_in, h in spans:
             def vm(*shape):
@@ -303,15 +314,16 @@
                 vm(2, 2),
                 vm(2, 4),
                 vm(3, 3),
-                vm(4, 2, 2),
+                vm(7, 2),
             ]
         n_chunk = len(spans)
         tall = -(-rows // 8) * 8
         scratch += [
             pltpu.SemaphoreType.DMA((n_chunk, 2)),
             pltpu.VMEM((4, 2, 2, slots * 16, LANES), F32),
-            pltpu.SemaphoreType.DMA((n_chunk, 23)),
-            pltpu.SemaphoreType.DMA((n_chunk, 23)),
+            pltpu.VMEM((8, LANES), F32),
+            pltpu.SemaphoreType.DMA((n_chunk, 25)),
+            pltpu.SemaphoreType.DMA((n_chunk, 25)),
             pltpu.VMEM((2, tall, LANES), F32),
             pltpu.VMEM((8, LANES), F32),
             pltpu.VMEM((years, 8, LANES), F32),
@@ -340,7 +352,20 @@
             compiler_params=pltpu.CompilerParams(
                 collective_id=0, has_side_effects=True, vmem_limit_bytes=60 * 2**20),
         )(filled_calendar, jnp.transpose(predicted_anomaly, (0, 1, 3, 2, 4)), jnp.transpose(measured_anomaly, (0, 1, 3, 2, 4)))
-        return bias[None, :, None, :], acc[:, None, :], rmse[:, None, :], scores
+        bias, acc, rmse, scores = pl.pallas_call(
+            place,
+            name="place_outputs",
+            out_shape=(
+                jax.ShapeDtypeStruct((rows, 1, band // years), F32),
+                jax.ShapeDtypeStruct((rows, 1, LANES), F32),
+                jax.ShapeDtypeStruct((rows, 1, LANES), F32),
+                jax.ShapeDtypeStruct((2, rows), F32),
+            ),
+            in_specs=[pl.BlockSpec(memory_space=pltpu.VMEM)] * 4,
+            out_specs=[pl.BlockSpec(memory_space=pl.ANY)] * 4,
+            scratch_shapes=[pltpu.SemaphoreType.DMA((4,))],
+        )(bias, acc, rmse, scores)
+        return bias[None], acc, rmse, scores
 
     return jax.shard_map(
         body,

time: 77.3 us -> 67.3 us (0.87)
  local copies, waits for them, and re-layouts: 6.2 us -> 0 us
  Pallas kernels: 69.6 us -> 65.9 us
    unnamed x4 -> x0, local copies, waits for them, and re-layouts: 6.2 us -> none
    pallas_call x1, Pallas kernels: 69.6 us -> 64.1 us  [body(): pl.pallas_call(functools.partial(kernel, rows, years, dates, band, spans,...]
    pallas_call x0 -> x1, Pallas kernels: none -> 1.8 us  [body(): pl.pallas_call(place, name='place_outputs', out_shape=(jax.ShapeDtypeStru...]
where the time goes in v3:
time: 67.3 us; the launch traced here: 67.2 us
  Pallas kernels  65.9 us (98%)
  between operations  1.29 us (2%)
    pallas_call x1, Pallas kernels, body(): pl.pallas_call(functools.partial(kernel, rows, years, dates, band, spans,...  64.1 us
    pallas_call x1, Pallas kernels, body(): pl.pallas_call(place, name='place_outputs', out_shape=(jax.ShapeDtypeStru...  1.8 us

profile of v3, /device:TPU:1, one launch (start us, length us, event | category | flops | bytes accessed | tf_op | source)
XLA Modules:
  0.0 67.2 jit_solution(16285098024086100795)
XLA Ops:
  1.3 64.1 %bias_and_maps.1 = (f32[83,1024]{1,0:T(8,128)}, f32[83,128]{1,0:T(8,128)}, f32[83,128]{1,0:T(8,128)}, f32[2,83]{1,0:T(2,128)}) custom-call(s32[1]{0:T(128)S(6)} %copy.7.count_ref, bf16[2,1,83,4,8192]{4,3,2,1,0:T(4,128)(2,1)} %bitcast.3, bf16[2,1,83,4,8192]{4,3,2,1,0:T(4,128)(2,1)} %bitcast.4), custom_call_target="tpu_custom_call" | custom-call | tf_op jit(solution)/shard_map/bias_and_maps/pallas_call | solution.py:336
  65.4 1.8 %place_outputs.1 = (f32[83,1,1024]{2,1,0:T(1,128)}, f32[83,1,128]{2,1,0:T(1,128)}, f32[83,1,128]{2,1,0:T(1,128)}, f32[2,83]{1,0:T(2,128)}) custom-call(f32[83,1024]{1,0:T(8,128)} %get-tuple-element.12.bias, f32[83,128]{1,0:T(8,128)} %get-tuple-element.13.acc, f32[83,128]{1,0:T(8,128)} %get-tuple-element.14.rmse, f32[2,83]{1,0:T(2,128)} %get-tuple-element.15.score), custom_call_target="tpu_custom_call" | custom-call | tf_op jit(solution)/shard_map/place_outputs/pallas_call | solution.py:355

commit v4 on v3

--- a/solution.py
+++ b/solution.py
@@ -86,13 +86,12 @@
         for copy in arriving[i].pop(name):
             copy.wait_recv()
 
-    def local_sums(i, n):
+    def local_sums(i, n, m):
         fb, ob, w = bufs[i][0], bufs[i][1], bufs[i][2]
         height = spans[i][2]
         deep = fb.shape[1]
 
-        def step(km, carry):
-            k, m = km // 2, km % 2
+        def step(k, carry):
             base = ((((x + k) % 4) * 2 + (c + n) % 2) * 8 + ((zh + m) % 2) * 4) * LANES
             for j in range(4):
                 lanes = pl.ds(pl.multiple_of(base + ((y + j) % 4) * LANES, LANES), LANES)
@@ -112,44 +111,34 @@
                     both = [a + b for a, b in zip(*vals)]
                     totals = both if totals is None else [a + b for a, b in zip(totals, both)]
                 sf, so, ff, oo, ee = totals
-                w[n, E, k, m, j] = sf - so
-                w[n, T, k, m, j] = sf + so
-                w[n, OO, k, m, j] = oo
-                w[n, FF, k, m, j] = ff
-                w[n, EE, k, m, j] = ee
+                for q, value in ((E, sf - so), (T, sf + so), (OO, oo), (FF, ff), (EE, ee)):
+                    w[n, q, k, m, j] = value if n else value + bufs[i][3][q, k, m, j]
             return carry
 
-        lax.fori_loop(0, 8, step, 0)
+        lax.fori_loop(0, 4, step, 0)
 
     def stage0(i):
         w, dr = bufs[i][2], bufs[i][3]
         loaded(i)
-        local_sums(i, 1)
-        if i == 0:
-            pl.semaphore_wait(barrier, years - 1 + 2 * dates - 1)
-        send(i, "core", w.at[1], dr, device(dc=1))
+        for m in (1, 0):
+            local_sums(i, 1, m)
+            if i == 0 and m == 1:
+                pl.semaphore_wait(barrier, years - 1 + 2 * dates - 1)
+            send(i, "core%d" % m, w.at[1, :, :, m], dr.at[:, :, m], device(dc=1))
         if i + 2 < n_chunk:
             load(i + 2, 0)
             load(i + 2, 1)
 
-    def stage0b(i):
-        local_sums(i, 0)
 
     def stage1(i):
         (_, _, w, dr, x1, x2, y1e, y2e, ze, za, y1a, y2a, xq, late) = bufs[i]
-        arrive(i, "core")
-
-        def add(qk, carry):
-            q, k = qk // 4, qk % 4
-            w[0, q, k] = w[0, q, k] + dr[q, k]
-            return carry
-
-        lax.fori_loop(0, 20, add, 0)
-        for h, way in enumerate((1, 3)):
-            send(i, "x1", w.at[0, 0:2, 2, h], x1.at[h], device(dx=way))
-        for h, way in enumerate((1, 3)):
-            send(i, "y1e", w.at[0, 3:5, 1:4, h, 2], y1e.at[h], device(dy=way))
-        send(i, "za", w.at[0, OO, :, 1], za, device(dz=1))
+        for m, way in ((1, 3), (0, 1)):
+            arrive(i, "core%d" % m)
+            local_sums(i, 0, m)
+            if m == 1:
+                send(i, "za", w.at[0, OO, :, 1], za, device(dz=1))
+            send(i, "x1", w.at[0, 0:2, 2, m], x1.at[m], device(dx=way))
+            send(i, "y1e", w.at[0, 3:5, 1:4, m, 2], y1e.at[m], device(dy=way))
 
     def stage2(i):
         (_, _, w, dr, x1, x2, y1e, y2e, ze, za, y1a, y2a, xq, late) = bufs[i]
@@ -219,7 +208,7 @@
         maps[0, pl.ds(first, height), :] = acc
         maps[1, pl.ds(first, height), :] = rmse
 
-    order = ((stage0, 0), (stage1, 1), (stage0b, 0), (stage2, 2), (stage3, 3), (stage4, 4), (stage5, 5))
+    order = ((stage0, 0), (stage1, 1), (stage2, 2), (stage3, 3), (stage4, 4), (stage5, 5))
     for turn in range(n_chunk + max(lag for _, lag in order)):
         for stage, lag in order:
             if 0 <= turn - lag < n_chunk:
@@ -235,7 +224,7 @@
     mine[...] = jnp.zeros_like(mine)
     mine[:, 0:sums[0].shape[1]] = jnp.where(is_acc, sums[0], sums[1])
 
-    def exchange(own, group, ssem, rsem, me, n, target):
+    def exchange(own, group, ssem, rsem, me, n, target, hidden=()):
         copies = []
         for d in range(1, n):
             copy = pltpu.make_async_remote_copy(
@@ -244,6 +233,8 @@
             copy.start()
             copies.append(copy)
         group[me] = own[...]
+        for copy in hidden:
+            copy.wait_send()
         for d in range(1, n):
             other = (me + d) % n
             pltpu.make_async_remote_copy(
@@ -256,7 +247,8 @@
             total = total + group[d]
         return total
 
-    own_sum = exchange(mine.at[0:8], group_a, sa_sem, ra_sem, yr, years, lambda d: ((yr + d) % years, dt, px))
+    own_sum = exchange(mine.at[0:8], group_a, sa_sem, ra_sem, yr, years, lambda d: ((yr + d) % years, dt, px),
+                       [copy for copies in sent for copy in copies])
     mine[...] = own_sum
     place = dt * 2 + px
 
@@ -266,9 +258,6 @@
 
     total = exchange(mine.at[0:8], group_b, sb_sem, rb_sem, place, 2 * dates, in_group_b)
     score_ref[...] = total[0:2, 0:rows] * (1.0 / weight_total)
-    for i in range(n_chunk):
-        for copy in sent[i]:
-            copy.wait_send()
 
 
 def place(bias, acc, rmse, score, bias_out, acc_out, rmse_out, score_out, sem):
@@ -320,10 +309,10 @@
         tall = -(-rows // 8) * 8
         scratch += [
             pltpu.SemaphoreType.DMA((n_chunk, 2)),
-            pltpu.VMEM((4, 2, 2, slots * 16, LANES), F32),
+            pltpu.VMEM((4, 2, 2, -(-slots * max(h for _, _, h in spans) // 16) * 16, LANES), F32),
             pltpu.VMEM((8, LANES), F32),
-            pltpu.SemaphoreType.DMA((n_chunk, 25)),
-            pltpu.SemaphoreType.DMA((n_chunk, 25)),
+            pltpu.SemaphoreType.DMA((n_chunk, 26)),
+            pltpu.SemaphoreType.DMA((n_chunk, 26)),
             pltpu.VMEM((2, tall, LANES), F32),
             pltpu.VMEM((8, LANES), F32),
             pltpu.VMEM((years, 8, LANES), F32),

time: 67.3 us -> 66.5 us (0.988)
  Pallas kernels: 65.9 us -> 65.1 us
    pallas_call x1, Pallas kernels: 64.1 us -> 63.3 us  [body(): pl.pallas_call(functools.partial(kernel, rows, years, dates, band, spans,...]
where the time goes in v4:
time: 66.5 us; the launch traced here: 66.4 us
  Pallas kernels  65.1 us (98%)
  between operations  1.29 us (2%)
    pallas_call x1, Pallas kernels, body(): pl.pallas_call(functools.partial(kernel, rows, years, dates, band, spans,...  63.3 us
    pallas_call x1, Pallas kernels, body(): pl.pallas_call(place, name='place_outputs', out_shape=(jax.ShapeDtypeStru...  1.8 us

profile of v4, /device:TPU:1, one launch (start us, length us, event | category | flops | bytes accessed | tf_op | source)
XLA Modules:
  0.0 66.4 jit_solution(8275713376579720089)
XLA Ops:
  1.3 63.3 %bias_and_maps.1 = (f32[83,1024]{1,0:T(8,128)}, f32[83,128]{1,0:T(8,128)}, f32[83,128]{1,0:T(8,128)}, f32[2,83]{1,0:T(2,128)}) custom-call(s32[1]{0:T(128)S(6)} %copy.7.count_ref, bf16[2,1,83,4,8192]{4,3,2,1,0:T(4,128)(2,1)} %bitcast.3, bf16[2,1,83,4,8192]{4,3,2,1,0:T(4,128)(2,1)} %bitcast.4), custom_call_target="tpu_custom_call" | custom-call | tf_op jit(solution)/shard_map/bias_and_maps/pallas_call | solution.py:325
  64.6 1.8 %place_outputs.1 = (f32[83,1,1024]{2,1,0:T(1,128)}, f32[83,1,128]{2,1,0:T(1,128)}, f32[83,1,128]{2,1,0:T(1,128)}, f32[2,83]{1,0:T(2,128)}) custom-call(f32[83,1024]{1,0:T(8,128)} %get-tuple-element.12.bias, f32[83,128]{1,0:T(8,128)} %get-tuple-element.13.acc, f32[83,128]{1,0:T(8,128)} %get-tuple-element.14.rmse, f32[2,83]{1,0:T(2,128)} %get-tuple-element.15.score), custom_call_target="tpu_custom_call" | custom-call | tf_op jit(solution)/shard_map/place_outputs/pallas_call | solution.py:344

commit v5 on v4

--- a/solution.py
+++ b/solution.py
@@ -160,6 +160,10 @@
     def stage3(i):
         (_, _, w, dr, x1, x2, y1e, y2e, ze, za, y1a, y2a, xq, late) = bufs[i]
         first, high, height = spans[i]
+        arrive(i, "y2e")
+        for m in range(2):
+            w[0, 3:5, 1:4, m, 0] = w[0, 3:5, 1:4, m, 0] + y2e[0, :, :, m] + y2e[1, :, :, m]
+        send(i, "ze", w.at[0, 3:5, 1:4, 1, 0], ze, device(dz=1))
         arrive(i, "x2")
         for m in range(2):
             for j in range(4):
@@ -172,10 +176,6 @@
                 w[0, EE, 0, m, j] = w[0, EE, 0, m, j] - b * e
         for r in range(1, 8):
             send(i, "late", w.at[0, 3:5, 0, r // 4, r % 4], late.at[r - 1], device(dy=r % 4, dz=r // 4))
-        arrive(i, "y2e")
-        for m in range(2):
-            w[0, 3:5, 1:4, m, 0] = w[0, 3:5, 1:4, m, 0] + y2e[0, :, :, m] + y2e[1, :, :, m]
-        send(i, "ze", w.at[0, 3:5, 1:4, 1, 0], ze, device(dz=1))
         arrive(i, "y1a")
         w[0, OO, 0:2, 0, 1] = w[0, OO, 0:2, 0, 1] + y1a[0]
         w[0, OO, 2:4, 0, 3] = w[0, OO, 2:4, 0, 3] + y1a[1]

time: 66.5 us -> 66.2 us (level)
  no operation moved by 1% of the time
where the time goes in v5:
time: 66.2 us; the launch traced here: 66 us
  Pallas kernels  64.8 us (98%)
  between operations  1.29 us (2%)
    pallas_call x1, Pallas kernels, body(): pl.pallas_call(functools.partial(kernel, rows, years, dates, band, spans,...  63 us
    pallas_call x1, Pallas kernels, body(): pl.pallas_call(place, name='place_outputs', out_shape=(jax.ShapeDtypeStru...  1.8 us

profile of v5, /device:TPU:1, one launch (start us, length us, event | category | flops | bytes accessed | tf_op | source)
XLA Modules:
  0.0 66.0 jit_solution(15801629389484140708)
XLA Ops:
  1.3 63.0 %bias_and_maps.1 = (f32[83,1024]{1,0:T(8,128)}, f32[83,128]{1,0:T(8,128)}, f32[83,128]{1,0:T(8,128)}, f32[2,83]{1,0:T(2,128)}) custom-call(s32[1]{0:T(128)S(6)} %copy.7.count_ref, bf16[2,1,83,4,8192]{4,3,2,1,0:T(4,128)(2,1)} %bitcast.3, bf16[2,1,83,4,8192]{4,3,2,1,0:T(4,128)(2,1)} %bitcast.4), custom_call_target="tpu_custom_call" | custom-call | tf_op jit(solution)/shard_map/bias_and_maps/pallas_call | solution.py:325
  64.2 1.8 %place_outputs.1 = (f32[83,1,1024]{2,1,0:T(1,128)}, f32[83,1,128]{2,1,0:T(1,128)}, f32[83,1,128]{2,1,0:T(1,128)}, f32[2,83]{1,0:T(2,128)}) custom-call(f32[83,1024]{1,0:T(8,128)} %get-tuple-element.12.bias, f32[83,128]{1,0:T(8,128)} %get-tuple-element.13.acc, f32[83,128]{1,0:T(8,128)} %get-tuple-element.14.rmse, f32[2,83]{1,0:T(2,128)} %get-tuple-element.15.score), custom_call_target="tpu_custom_call" | custom-call | tf_op jit(solution)/shard_map/place_outputs/pallas_call | solution.py:344
